TPU v7x, 256 devices: a whole 4x4x8 slice. The times are simulated.
256 devices in a mesh: batch: 8 (over x, core), slab: 32 (over y, z).
Axes of the slice: x: 4, y: 4, z: 8, core: 2. Of those that a mesh axis runs over, the one named last changes fastest.
Arguments:
- volume: bfloat16 [8, 32, 128, 16, 128], P('batch', None, 'slab'), may hold values from -6 to 6
- kernel: bfloat16 [32, 32, 3, 3, 3], replicated, may hold values from -0.21875 to 0.21875
- offset: float32 [32], replicated, may hold values from -1 to 1
- upstream: bfloat16 [8, 32, 128, 16, 128], P('batch', None, 'slab'), may hold values from -6 to 6
Outputs:
- activated: bfloat16 [8, 32, 128, 16, 128], P('batch', None, 'slab')
- grad_volume: bfloat16 [8, 32, 128, 16, 128], P('batch', None, 'slab')
- grad_kernel: float32 [32, 32, 3, 3, 3], replicated
- grad_offset: float32 [32], replicated
All inputs are finite; a program needn't handle non-finite values.
Results may differ from a plain program's by a relative error of at most 0.0085.
Values may be sent and summed in bfloat16 or wider, within the bound.
A program may use at most 64 MiB of HBM per device.

v0:
```python
import jax
import jax.numpy as jnp
from jax import lax
from jax.sharding import PartitionSpec as P


def padded_2(block, sides, width):
    for axis, dim in sides:
        count = lax.axis_size(axis)
        forward = [(i, i + 1) for i in range(count - 1)]
        backward = [(target, source) for source, target in forward]
        low = lax.ppermute(
            lax.slice_in_dim(block, block.shape[dim] - width, None, axis=dim), axis, forward
        )
        high = lax.ppermute(lax.slice_in_dim(block, 0, width, axis=dim), axis, backward)
        block = jnp.concatenate([low, block, high], axis=dim)
    return block


def convolve_depth(field, weights):
    return lax.conv_general_dilated(
        field,
        weights,
        (1, 1, 1),
        ((0, 0), (1, 1), (1, 1)),
        dimension_numbers=("NCDHW", "OIDHW", "NCDHW"),
        preferred_element_type=jnp.float32,
    )


def pre_gradient(preact, cotangent):
    sig = jax.nn.sigmoid(preact)
    output = (preact * sig).astype(jnp.bfloat16)
    grad_pre = (cotangent.astype(jnp.float32) * sig * (1.0 + preact * (1.0 - sig))).astype(
        jnp.bfloat16
    )
    return (output, grad_pre)


def kernel_terms(haloed, grad_pre, planes):
    rows, cols = (grad_pre.shape[3], grad_pre.shape[4])
    padded = jnp.pad(haloed, ((0, 0), (0, 0), (0, 0), (1, 1), (1, 1)))
    terms = []
    for first in range(3):
        for second in range(3):
            for third in range(3):
                window = padded[
                    :, :, first : first + planes, second : second + rows, third : third + cols
                ]
                terms.append(
                    jnp.einsum(
                        "nodhw,nidhw->oi", grad_pre, window, preferred_element_type=jnp.float32
                    )
                )
    return jnp.stack(terms, axis=2)


def on_device(volume, kernel, offset, upstream):
    planes = volume.shape[2]
    flipped = jnp.transpose(jnp.flip(kernel, (2, 3, 4)), (1, 0, 2, 3, 4))
    bias = offset[None, :, None, None, None]
    haloed = padded_2(volume, (("slab", 2),), 1)
    preact = convolve_depth(haloed, kernel) + bias
    activated, grad_pre = pre_gradient(preact, upstream)
    grad_haloed = padded_2(grad_pre, (("slab", 2),), 1)
    grad_volume = convolve_depth(grad_haloed, flipped).astype(jnp.bfloat16)
    local_kernel = kernel_terms(haloed, grad_pre, planes).reshape(kernel.shape)
    local_offset = jnp.sum(grad_pre.astype(jnp.float32), axis=(0, 2, 3, 4))
    summed_kernel, summed_offset = lax.psum((local_kernel, local_offset), ("batch", "slab"))
    cells = (
        volume.shape[0]
        * planes
        * volume.shape[3]
        * volume.shape[4]
        * lax.axis_size("batch")
        * lax.axis_size("slab")
    )
    scale = 1.0 / jnp.sqrt(jnp.float32(cells))
    return (activated, grad_volume, summed_kernel * scale, summed_offset * scale)


def solution(mesh):
    placed = (P("batch", None, "slab", None, None), P(), P(), P("batch", None, "slab", None, None))
    return jax.shard_map(
        on_device,
        mesh=mesh,
        in_specs=placed,
        out_specs=(
            P("batch", None, "slab", None, None),
            P("batch", None, "slab", None, None),
            P(),
            P(),
        ),
        check_vma=False,
    )
```

profile of v0, /device:TPU:1, one launch (start us, length us, event | category | flops | bytes accessed | tf_op | source)
XLA Modules:
  0.0 333.9 jit_solution(11143610916050945041)
XLA Ops:
  7.2 0.0 all-reduce.3.cloned.1.call-start
  7.2 1.4 copy.135
  8.7 4.4 %collective-permute-start = (bf16[1,32,1,16,128]{4,1,3,2,0:T(8,128)(2,1)S(1)}, bf16[1,32,1,16,128]{4,1,3,2,0:T(8,128)(2,1)S(1)}, u32[]{:S(2)}, u32[]{:S(2)}) collective-permute-start(bf16[1,32,1,16,128]{4,1,3,2,0:T(8,128)(2,1)S(1)} %get-tuple-element.24), channel_id=1, source_target_pairs={{0,1},{1,2},{2,3},{3,4},{4,5},{5,6},{6,7},{7,8},{8,9},{9,10},{10,1... | collective-permute-start | bytes 393224 | tf_op jit(solution)/shard_map/ppermute | solution.py:12
  13.1 1.3 collective-permute-start.1
  14.4 3.2 copy.142
  17.6 1.5 constant_dynamic-update-slice_fusion.1
  19.1 0.3 collective-permute-done.1
  19.4 3.4 %copy.207 = bf16[32,6,16,1,128]{0,2,4,1,3:T(8,128)(2,1)} copy(bf16[32,6,16,1,128]{4,0,2,1,3:T(8,128)(2,1)S(1)} %bitcast.363) | data formatting | bytes 1572864
  22.8 2.5 pad.5.clone
  25.4 0.9 copy.140
  26.3 0.1 slice.134
  26.4 8.8 %add_divide_fusion = (f32[4,16,8,17,32]{4,2,3,1,0:T(8,128)S(1)}, bf16[4,16,8,17,32]{4,2,3,1,0:T(8,128)(2,1)S(1)}, f32[4,16,8,17,32]{4,2,3,1,0:T(8,128)S(1)}) fusion(f32[32]{0:T(128)S(1)} %copy-done.10, pred[8,17]{0,1:T(8,128)(4,1)S(1)} %copy-done.11, bf16[32,32,3,3,3]{1,0,4,3,2:T(8,128)(2,1)S(1)} %copy-done, bf16[32,6,16,1,7,2]{0,4,5,2,1,3:T(8,128)(2,1)S(1)} %slice.134, ...), kind=kOutput, calls=%fused_computation.30 | convolution fusion | flops 466829312 | bytes 3762440 | tf_op jit(solution)/shard_map/conv_general_dilated | solution.py:21
  35.3 0.4 copy.141
  35.6 1.7 slice_bitcast_fusion.3
  37.3 0.8 copy.144
  38.1 1.0 copy.143
  39.1 1.3 convert_reduce_fusion
  40.4 0.2 fusion.138
  40.6 1.1 copy-done.1
  41.7 2.8 copy.148
  44.6 0.4 fusion.49
  44.9 0.3 fusion.48
  45.2 0.4 fusion.47
  45.6 0.4 fusion.46
  45.9 0.3 fusion.45
  46.2 0.4 fusion.44
  46.6 0.4 fusion.43
  46.9 0.3 fusion.42
  47.2 0.4 fusion.41
  47.6 0.4 fusion.40
  47.9 0.3 fusion.39
  48.2 0.4 fusion.38
  48.6 0.4 fusion.37
  49.0 0.5 fusion.36
  49.4 0.4 fusion.35
  49.8 0.4 fusion.34
  50.1 0.3 fusion.33
  50.4 0.4 fusion.32
  50.8 0.4 fusion.31
  51.2 0.3 fusion.30
  51.4 0.4 fusion.29
  51.8 0.4 fusion.28
  52.2 0.3 fusion.27
  52.4 0.4 fusion.26
  52.8 0.4 fusion.25
  53.2 0.3 fusion.24
  53.4 0.4 fusion.23
  53.8 0.8 copy-done.5
  54.6 0.0 all-reduce.3.cloned.1.call-update
  54.6 81.2 %psum.15 = f32[32]{0:T(128)S(1)} all-reduce(f32[32]{0:T(128)S(1)} %get-tuple-element.16), channel_id=1, replica_groups=mesh['batch'=8,'slab'=32] {'batch','slab'}, use_global_device_ids=true, to_apply=%region_2.3 | all-reduce | flops 32 | bytes 256 | tf_op jit(solution)/shard_map/psum | solution.py:69
  135.8 0.5 broadcast_multiply_fusion.1
  136.3 4.0 %copy.178 = bf16[1,32,4,16,128]{4,3,2,1,0:T(8,128)(2,1)} copy(bf16[1,32,4,16,128]{1,3,4,2,0:T(8,128)(2,1)} %slice_bitcast_fusion.3) | data formatting | bytes 1048576
  140.3 1.3 collective-permute-start.3
  141.6 4.3 %collective-permute-start.2 = (bf16[1,32,1,16,128]{1,3,4,2,0:T(8,128)(2,1)S(1)}, bf16[1,32,1,16,128]{1,3,4,2,0:T(8,128)(2,1)S(1)}, u32[]{:S(2)}, u32[]{:S(2)}) collective-permute-start(bf16[1,32,1,16,128]{1,3,4,2,0:T(8,128)(2,1)S(1)} %get-tuple-element.21), channel_id=1, source_target_pairs={{0,1},{1,2},{2,3},{3,4},{4,5},{5,6},{6,7},{7,8},{8,9},{9,10},{10,1... | collective-permute-start | bytes 393224 | tf_op jit(solution)/shard_map/ppermute | solution.py:12
  145.8 164.6 %all-reduce.3.cloned.1.call-done = f32[32,32,3,3,3]{1,0,4,3,2:T(8,128)} async-done(((f32[32,32,3,3,3]{1,0,4,3,2:T(8,128)}), f32[32,32,3,3,3]{1,0,4,3,2:T(8,128)}) %all-reduce.3.cloned.1.call-update) | async-done | bytes 110608 | tf_op jit(solution)/shard_map/psum | solution.py:69
  310.4 1.8 broadcast_multiply_fusion
  312.3 2.3 maximum_bitcast_fusion
  314.6 0.6 pad.7
  315.2 0.9 copy.146
  316.1 0.1 slice.140
  316.2 7.2 %select_convert_fusion = bf16[4,16,8,17,32]{4,2,3,1,0:T(8,128)(2,1)S(1)} fusion(pred[8,17]{0,1:T(8,128)(4,1)S(1)} %copy-done.11, bf16[32,32,3,3,3]{1,0,4,3,2:T(8,128)(2,1)S(1)} %copy-done, bf16[32,6,16,1,7,2]{0,4,5,2,1,3:T(8,128)(2,1)S(1)} %slice.140, bf16[32,6,16,1,8,17]{0,4,5,2,1,3:T(8,128)(2,1)S(1)} %copy.146), kind=kOutput, calls=%fused_computation.27 | convolution fusion | flops 464601088 | bytes 1534088 | tf_op jit(solution)/shard_map/conv_general_dilated | solution.py:21
  323.4 0.4 copy.147
  323.8 0.4 slice_bitcast_fusion.2
  324.2 2.9 copy.179
  (28 shorter events, 0.1 us)
Async XLA Ops:
  7.2 19.2 %copy-start = (bf16[32,32,3,3,3]{1,0,4,3,2:T(8,128)(2,1)S(1)}, bf16[32,32,3,3,3]{1,0,4,3,2:T(8,128)(2,1)}, u32[]{:S(2)}) copy-start(bf16[32,32,3,3,3]{1,0,4,3,2:T(8,128)(2,1)} %param.5) | copy-start | bytes 165892
  7.2 303.3 %all-reduce.3.cloned.1.call-start = ((), (), s32[]{:S(2)}) async-start(), calls=%async_computation | async-start | bytes 884736 | tf_op jit(solution)/shard_map/psum | solution.py:69
  8.7 8.9 %copy-start.3 = (bf16[1,32,4,16,128]{4,1,3,2,0:T(8,128)(2,1)}, bf16[1,32,4,16,128]{4,1,3,2,0:T(8,128)(2,1)S(1)}, u32[]{:S(2)}) copy-start(bf16[1,32,4,16,128]{4,1,3,2,0:T(8,128)(2,1)S(1)} %copy.135) | copy-start | bytes 1572868
  8.7 8.9 %collective-permute-start = (bf16[1,32,1,16,128]{4,1,3,2,0:T(8,128)(2,1)S(1)}, bf16[1,32,1,16,128]{4,1,3,2,0:T(8,128)(2,1)S(1)}, u32[]{:S(2)}, u32[]{:S(2)}) collective-permute-start(bf16[1,32,1,16,128]{4,1,3,2,0:T(8,128)(2,1)S(1)} %get-tuple-element.24), channel_id=1, source_target_pairs={{0,1},{1,2},{2,3},{3,4},{4,5},{5,6},{6,7},{7,8},{8,9},{9,10},{10,1... | collective-permute-start | bytes 393224 | tf_op jit(solution)/shard_map/ppermute | solution.py:12
  13.1 6.3 %collective-permute-start.1 = (bf16[1,32,1,16,128]{4,1,3,2,0:T(8,128)(2,1)S(1)}, bf16[1,32,1,16,128]{4,1,3,2,0:T(8,128)(2,1)S(1)}, u32[]{:S(2)}, u32[]{:S(2)}) collective-permute-start(bf16[1,32,1,16,128]{4,1,3,2,0:T(8,128)(2,1)S(1)} %get-tuple-element.23), channel_id=1, source_target_pairs={{1,0},{2,1},{3,2},{4,3},{5,4},{6,5},{7,6},{8,7},{9,8},{10,9},{11,1... | collective-permute-start | bytes 393224 | tf_op jit(solution)/shard_map/ppermute | solution.py:15
  17.6 7.7 %copy-start.8 = (bf16[1,32,1,16,128]{4,1,3,2,0:T(8,128)(2,1)}, bf16[1,32,1,16,128]{4,1,3,2,0:T(8,128)(2,1)S(1)}, u32[]{:S(2)}) copy-start(bf16[1,32,1,16,128]{4,1,3,2,0:T(8,128)(2,1)S(1)} %collective-permute-done) | copy-start | bytes 393220
  19.4 6.0 %copy-start.6 = (bf16[1,32,1,16,128]{4,1,3,2,0:T(8,128)(2,1)}, bf16[1,32,1,16,128]{4,1,3,2,0:T(8,128)(2,1)S(1)}, u32[]{:S(2)}) copy-start(bf16[1,32,1,16,128]{4,1,3,2,0:T(8,128)(2,1)S(1)} %collective-permute-done.1) | copy-start | bytes 393220
  25.4 1.0 copy-start.10
  25.4 1.0 copy-start.11
  40.4 1.3 copy-start.1
  41.7 4.2 %copy-start.4 = (bf16[1,32,4,16,128]{4,1,3,2,0:T(8,128)(2,1)S(1)}, bf16[1,32,4,16,128]{4,1,3,2,0:T(8,128)(2,1)}, u32[]{:S(2)}) copy-start(bf16[1,32,4,16,128]{4,1,3,2,0:T(8,128)(2,1)} %copy-done.3) | copy-start | bytes 1572868
  44.5 1.4 copy-start.9
  47.2 1.7 copy-start.2
  50.4 1.7 copy-start.7
  53.8 0.8 copy-start.5
  140.3 172.0 %collective-permute-start.3 = (bf16[1,32,1,16,128]{1,3,4,2,0:T(8,128)(2,1)S(1)}, bf16[1,32,1,16,128]{1,3,4,2,0:T(8,128)(2,1)S(1)}, u32[]{:S(2)}, u32[]{:S(2)}) collective-permute-start(bf16[1,32,1,16,128]{1,3,4,2,0:T(8,128)(2,1)S(1)} %get-tuple-element.22), channel_id=1, source_target_pairs={{1,0},{2,1},{3,2},{4,3},{5,4},{6,5},{7,6},{8,7},{9,8},{10,9},{11,1... | collective-permute-start | bytes 393224 | tf_op jit(solution)/shard_map/ppermute | solution.py:15
  141.6 170.7 %collective-permute-start.2 = (bf16[1,32,1,16,128]{1,3,4,2,0:T(8,128)(2,1)S(1)}, bf16[1,32,1,16,128]{1,3,4,2,0:T(8,128)(2,1)S(1)}, u32[]{:S(2)}, u32[]{:S(2)}) collective-permute-start(bf16[1,32,1,16,128]{1,3,4,2,0:T(8,128)(2,1)S(1)} %get-tuple-element.21), channel_id=1, source_target_pairs={{0,1},{1,2},{2,3},{3,4},{4,5},{5,6},{6,7},{7,8},{8,9},{9,10},{10,1... | collective-permute-start | bytes 393224 | tf_op jit(solution)/shard_map/ppermute | solution.py:12
Sparse Core Ops, SparseCore 0:
  54.7 255.6 all-reduce.2
where the time goes:
time: 334 us
  waiting for transfers between devices  165 us (49%)
  blocking collectives  81.2 us (24%)
  local copies, waits for them, and re-layouts  31 us (9%)
  matrix products  25.2 us (8%)
  between operations  14.4 us (4%)
  starting transfers between devices  11.3 us (3%)
  other arithmetic  5.9 us (2%)
    psum x1, waiting for transfers between devices, on_device(): lax.psum((local_kernel, local_offset), ('batch', 'slab'))  165 us
    psum x1, blocking collectives, on_device(): lax.psum((local_kernel, local_offset), ('batch', 'slab'))  81.2 us
    unnamed x31, local copies, waits for them, and re-layouts  18.4 us
    conv_general_dilated x2, matrix products, convolve_depth(): lax.conv_general_dilated(field, weights, (1, 1, 1), ((0, 0), (1, 1), (1,...  16.1 us
    dot_general x27, matrix products, kernel_terms(): jnp.einsum('nodhw,nidhw->oi', grad_pre, window, preferred_element_type=jn...  9.17 us
    ppermute x2, starting transfers between devices, padded_2(): lax.ppermute(lax.slice_in_dim(block, block.shape[dim] - width, None, axis...  8.66 us
  transfers between devices with their start and end apart: 5, of which 2 were waited for; matrix products, arithmetic and copies ran while one was open for 3% of the time, Pallas kernels for 0%

commit v1 on v0

v1 whole, which is shorter than its diff:
```python
import functools

import jax
import jax.numpy as jnp
from jax import lax
from jax.experimental import pallas as pl
from jax.experimental.pallas import tpu as pltpu
from jax.sharding import PartitionSpec as P

MESH = pl.DeviceIdType.MESH
CH = 32
PLANES = 4
ROWS = 16
COLS = 128
BLOCK = 8
WIN = BLOCK + 2
TAPS = 3 * CH
DEEP = 3 * WIN * TAPS
GROUPS = 4
RING = 8


def banded(base, out_ref):
    for row in range(BLOCK):
        move = row * TAPS
        if move == 0:
            block = base
        else:
            block = jnp.concatenate([base[:, DEEP - move :], base[:, : DEEP - move]], axis=1)
        out_ref[row * CH : (row + 1) * CH, :] = block.astype(jnp.bfloat16)


def base_of(pieces):
    gap = jnp.zeros((CH, (WIN - 3) * TAPS), jnp.float32)
    parts = []
    for plane in pieces:
        parts.extend(plane)
        parts.append(gap)
    return jnp.concatenate(parts, axis=1)


def shifted(values, out_ref, slot, row, flip):
    lane = lax.broadcasted_iota(jnp.int32, (CH, COLS), 1)
    left = jnp.where(lane == 0, 0.0, pltpu.roll(values, 1, 1))
    right = jnp.where(lane == COLS - 1, 0.0, pltpu.roll(values, COLS - 1, 1))
    if flip:
        left, right = right, left
    out_ref[slot, row + 1, 0:CH, :] = left.astype(jnp.bfloat16)
    out_ref[slot, row + 1, CH : 2 * CH, :] = values.astype(jnp.bfloat16)
    out_ref[slot, row + 1, 2 * CH : 3 * CH, :] = right.astype(jnp.bfloat16)


def clear_edges(ref):
    zero = jnp.zeros((TAPS, COLS), jnp.bfloat16)
    for slot in range(PLANES + 2):
        ref[slot, 0] = zero
        ref[slot, ROWS + 1] = zero


def window(ref, slot, half):
    return ref[slot, half * BLOCK : half * BLOCK + WIN].reshape(WIN * TAPS, COLS)


def convolve(src_ref, t_ref, pair, out_ref):
    for half in range(ROWS // BLOCK):
        sides = []
        for slot in pair:
            sides.append(
                jnp.concatenate([window(src_ref, slot + s - 1, half) for s in range(3)], axis=0)
            )
        acc = jnp.dot(
            t_ref[...], jnp.concatenate(sides, axis=1), preferred_element_type=jnp.float32
        )
        for row in range(BLOCK):
            for side in range(2):
                out_ref[side, pl.ds(half * BLOCK + row, CH, stride=ROWS), :] = acc[
                    row * CH : (row + 1) * CH, side * COLS : (side + 1) * COLS
                ]


def weight_terms(gs_ref, xs_ref, pair, dacc_ref, first):
    lane = lax.broadcasted_iota(jnp.int32, (TAPS, COLS), 1) // CH
    for s in range(3):
        total = [None] * 3
        for half in range(ROWS // BLOCK):
            lhs = jnp.concatenate([window(gs_ref, slot, half) for slot in pair], axis=1)
            rhs = jnp.concatenate(
                [
                    xs_ref[
                        slot + s - 1, 1 + half * BLOCK : 1 + half * BLOCK + BLOCK, CH : 2 * CH, :
                    ].reshape(BLOCK * CH, COLS)
                    for slot in pair
                ],
                axis=1,
            )
            prod = lax.dot_general(
                lhs, rhs, (((1,), (1,)), ((), ())), preferred_element_type=jnp.float32
            )
            for kh in range(3):
                for quad in range(2):
                    picked = None
                    for block in range(4):
                        row = quad * 4 + block + 2 - kh
                        value = prod[row * TAPS : (row + 1) * TAPS, quad * COLS : (quad + 1) * COLS]
                        picked = value if picked is None else jnp.where(lane == block, value, picked)
                    total[kh] = picked if total[kh] is None else total[kh] + picked
        for kh in range(3):
            at = pl.ds((s * 3 + kh) * TAPS, TAPS)
            if first:
                dacc_ref[at, :] = total[kh]
            else:
                dacc_ref[at, :] += total[kh]


def body(
    comm,
    scale,
    vol,
    w_ref,
    off_ref,
    up,
    act,
    gvol,
    gk_ref,
    go_ref,
    vown,
    vhalo,
    upn,
    actn,
    gvn,
    xf,
    xs,
    gs,
    tf,
    tb,
    pre,
    dacc,
    oacc,
    pay,
    recv1,
    red,
    recv2,
    res,
    local_sem,
    vsend,
    vrecv,
    gsend,
    grecv,
    rsend,
    rrecv,
):
    if comm:
        batch, slab = lax.axis_index("batch"), lax.axis_index("slab")
        y, z = slab // RING, slab % RING
        members = 8 * GROUPS
        mine = batch * GROUPS + y
        above = (slab + 1) % (GROUPS * RING)
        below = (slab + GROUPS * RING - 1) % (GROUPS * RING)

        def group_peer(i):
            other = (mine + i) % members
            return other, (other // GROUPS, (other % GROUPS) * RING + z)

        def ring_peer(i):
            other = (z + i) % RING
            return other, (batch, y * RING + other)

    load_v = pltpu.make_async_copy(vol, vown, local_sem.at[0])
    load_v.start()
    load_u = pltpu.make_async_copy(up, upn, local_sem.at[1])
    load_u.start()

    if comm:
        barrier = pltpu.get_barrier_semaphore()
        for slot in (above, below):
            pl.semaphore_signal(barrier, 1, device_id=(batch, slot), device_id_type=MESH)

        def greet_ring(i, carry):
            pl.semaphore_signal(barrier, 1, device_id=ring_peer(i)[1], device_id_type=MESH)
            return carry

        def greet_group(i, carry):
            pl.semaphore_signal(barrier, 1, device_id=group_peer(i)[1], device_id_type=MESH)
            return carry

        lax.fori_loop(1, RING, greet_ring, 0)
        lax.fori_loop(1, members, greet_group, 0)
        pl.semaphore_wait(barrier, 2 + RING - 1 + members - 1)
        up_copy = pltpu.make_async_remote_copy(
            vol.at[:, PLANES - 1], vhalo.at[0], vsend.at[0], vrecv.at[0], (batch, above), MESH
        )
        down_copy = pltpu.make_async_remote_copy(
            vol.at[:, 0], vhalo.at[1], vsend.at[1], vrecv.at[1], (batch, below), MESH
        )
        up_copy.start()
        down_copy.start()
        has_below = jnp.where(slab == 0, 0.0, 1.0)
        has_above = jnp.where(slab == GROUPS * RING - 1, 0.0, 1.0)

    clear_edges(xs)
    clear_edges(gs)
    taps = w_ref[...].astype(jnp.float32)
    pieces = [
        [
            jnp.concatenate(
                [taps[((s * 3 + u) * 3 + k) * CH : ((s * 3 + u) * 3 + k + 1) * CH] for k in range(3)],
                axis=1,
            )
            for u in range(3)
        ]
        for s in range(3)
    ]
    banded(base_of(pieces), tf)

    def spread_volume(slot, values):
        xf[slot] = values.astype(jnp.float32).reshape(CH * ROWS, COLS)
        for row in range(ROWS):
            shifted(xf[slot, pl.ds(row, CH, stride=ROWS), :], xs, slot, row, False)

    load_v.wait()
    for plane in range(PLANES):
        spread_volume(plane + 1, vown[:, plane])
    load_u.wait()

    def forward(pair, first):
        convolve(xs, tf, pair, pre)
        for side in range(2):
            plane = pair[side] - 1
            for ch in range(CH):
                at = pl.ds(ch * ROWS, ROWS)
                value = pre[side, at, :] + off_ref[ch]
                sig = 0.5 * jnp.tanh(0.5 * value) + 0.5
                actn[ch, plane] = (value * sig).astype(jnp.bfloat16)
                grad = upn[ch, plane].astype(jnp.float32) * sig * (1.0 + value * (1.0 - sig))
                grad = grad.astype(jnp.bfloat16).astype(jnp.float32)
                pre[side, at, :] = grad
                row = jnp.sum(grad, axis=0, keepdims=True)
                if first and side == 0:
                    oacc[ch : ch + 1, :] = row
                else:
                    oacc[ch : ch + 1, :] += row
            for row in range(ROWS):
                shifted(pre[side, pl.ds(row, CH, stride=ROWS), :], gs, plane + 1, row, True)

    forward((2, 3), True)
    weight_terms(gs, xs, (2, 3), dacc, True)

    if comm:
        up_copy.wait_recv()
        down_copy.wait_recv()
        spread_volume(0, vhalo[0].astype(jnp.float32) * has_below)
        spread_volume(PLANES + 1, vhalo[1].astype(jnp.float32) * has_above)
    else:
        xs[0] = jnp.zeros_like(xs[0])
        xs[PLANES + 1] = jnp.zeros_like(xs[0])
        gs[0] = jnp.zeros_like(xs[0])
        gs[PLANES + 1] = jnp.zeros_like(xs[0])

    forward((1, 4), False)
    store_a = pltpu.make_async_copy(actn, act, local_sem.at[2])
    store_a.start()
    if comm:

        def edge(slot):
            return gs.at[slot, 1 : ROWS + 1, CH : 2 * CH, :]

        gup = pltpu.make_async_remote_copy(
            edge(PLANES), edge(0), gsend.at[0], grecv.at[0], (batch, above), MESH
        )
        gdown = pltpu.make_async_remote_copy(
            edge(1), edge(PLANES + 1), gsend.at[1], grecv.at[1], (batch, below), MESH
        )
        gup.start()
        gdown.start()
    weight_terms(gs, xs, (1, 4), dacc, False)

    packed_rows = 27 * CH // 4
    lane = lax.broadcasted_iota(jnp.int32, (packed_rows, COLS), 1) // CH
    folded = dacc[...]
    folded = folded + pltpu.roll(folded, 2 * CH, 1)
    folded = folded + pltpu.roll(folded, CH, 1)
    packed = folded[:packed_rows]
    for block in range(1, 4):
        packed = jnp.where(
            lane == block, folded[block * packed_rows : (block + 1) * packed_rows], packed
        )
    chunks = packed_rows // 8
    pay[:chunks] = packed.reshape(chunks, 8, COLS)
    pay[chunks : chunks + 4] = oacc[...].reshape(4, 8, COLS)
    pay[chunks + 4 :] = jnp.zeros((32 - chunks - 4, 8, COLS), jnp.float32)

    if comm:

        def scatter(i, carry):
            other, peer = group_peer(i)
            pltpu.make_async_remote_copy(
                pay.at[other], recv1.at[mine], rsend.at[0], rrecv.at[0], peer, MESH
            ).start()
            return carry

        lax.fori_loop(1, members, scatter, 0)
        recv1[mine] = pay[mine]

    turned = taps.T
    pieces = [
        [
            turned[:, ((2 - s) * 3 + 2 - u) * TAPS : ((2 - s) * 3 + 2 - u + 1) * TAPS]
            for u in range(3)
        ]
        for s in range(3)
    ]
    banded(base_of(pieces), tb)

    def backward(pair):
        convolve(gs, tb, pair, pre)
        for side in range(2):
            plane = pair[side] - 1
            gvn[:, plane] = pre[side].reshape(CH, ROWS, COLS).astype(jnp.bfloat16)

    backward((2, 3))

    if comm:
        some = pl.ds(0, members - 1)
        pltpu.make_async_copy(pay.at[some], recv1.at[some], rrecv.at[0]).wait()
        red[...] = jnp.sum(recv1[...], axis=0) * scale

        def exchange(i, carry):
            other, peer = ring_peer(i)
            pltpu.make_async_remote_copy(
                red, recv2.at[z], rsend.at[1], rrecv.at[1], peer, MESH
            ).start()
            return carry

        lax.fori_loop(1, RING, exchange, 0)
        recv2[z] = red[...]

        gup.wait()
        gdown.wait()
        for slot, keep in ((0, has_below), (PLANES + 1, has_above)):
            for row in range(ROWS):
                value = gs[slot, row + 1, CH : 2 * CH, :].astype(jnp.float32) * keep
                shifted(value, gs, slot, row, True)

        few = pl.ds(0, RING - 1)
        pltpu.make_async_copy(recv2.at[few], recv2.at[few], rrecv.at[1]).wait()
        res[mine] = jnp.sum(recv2[...], axis=0)

        def gather(i, carry):
            other, peer = group_peer(i)
            pltpu.make_async_remote_copy(
                res.at[mine], res.at[mine], rsend.at[2], rrecv.at[2], peer, MESH
            ).start()
            return carry

        lax.fori_loop(1, members, gather, 0)
    else:
        res[...] = pay[...] * scale

    backward((1, 4))
    store_g = pltpu.make_async_copy(gvn, gvol, local_sem.at[3])
    store_g.start()

    if comm:
        pltpu.make_async_copy(pay.at[some], recv1.at[some], rrecv.at[2]).wait()
    full = res[:chunks].reshape(packed_rows, COLS)
    for block in range(4):
        moved = full if block == 0 else pltpu.roll(full, COLS - block * CH, 1)
        gk_ref[block * packed_rows : (block + 1) * packed_rows, :] = moved[:, :CH]
    biases = res[chunks : chunks + 4].reshape(CH, COLS)
    go_ref[...] = jnp.sum(biases.T, axis=0, keepdims=True)

    store_a.wait()
    store_g.wait()
    if comm:
        up_copy.wait_send()
        down_copy.wait_send()
        pltpu.make_async_copy(pay.at[some], recv1.at[some], rsend.at[0]).wait()
        pltpu.make_async_copy(recv2.at[few], recv2.at[few], rsend.at[1]).wait()
        pltpu.make_async_copy(pay.at[some], recv1.at[some], rsend.at[2]).wait()


def layer(comm, scale, volume, kernel, offset, upstream):
    taps = jnp.transpose(kernel, (2, 3, 4, 0, 1)).reshape(27 * CH, CH)
    shape = (CH, PLANES, ROWS, COLS)
    wide = (PLANES + 2, ROWS + 2, TAPS, COLS)
    half, full = jnp.bfloat16, jnp.float32
    hbm = pl.BlockSpec(memory_space=pl.ANY)
    vmem = pl.BlockSpec(memory_space=pltpu.VMEM)
    act, gvol, gk, go = pl.pallas_call(
        functools.partial(body, comm, scale),
        out_shape=(
            jax.ShapeDtypeStruct(shape, half),
            jax.ShapeDtypeStruct(shape, half),
            jax.ShapeDtypeStruct((27 * CH, CH), full),
            jax.ShapeDtypeStruct((1, CH), full),
        ),
        in_specs=[hbm, vmem, pl.BlockSpec(memory_space=pltpu.SMEM), hbm],
        out_specs=(hbm, hbm, vmem, vmem),
        scratch_shapes=[
            pltpu.VMEM(shape, half),
            pltpu.VMEM((2, CH, ROWS, COLS), half),
            pltpu.VMEM(shape, half),
            pltpu.VMEM(shape, half),
            pltpu.VMEM(shape, half),
            pltpu.VMEM((PLANES + 2, CH * ROWS, COLS), full),
            pltpu.VMEM(wide, half),
            pltpu.VMEM(wide, half),
            pltpu.VMEM((BLOCK * CH, DEEP), half),
            pltpu.VMEM((BLOCK * CH, DEEP), half),
            pltpu.VMEM((2, CH * ROWS, COLS), full),
            pltpu.VMEM((27 * CH, COLS), full),
            pltpu.VMEM((CH, COLS), full),
            pltpu.VMEM((32, 8, COLS), full),
            pltpu.VMEM((32, 8, COLS), full),
            pltpu.VMEM((8, COLS), full),
            pltpu.VMEM((RING, 8, COLS), full),
            pltpu.VMEM((32, 8, COLS), full),
            pltpu.SemaphoreType.DMA((4,)),
            pltpu.SemaphoreType.DMA((2,)),
            pltpu.SemaphoreType.DMA((2,)),
            pltpu.SemaphoreType.DMA((2,)),
            pltpu.SemaphoreType.DMA((2,)),
            pltpu.SemaphoreType.DMA((3,)),
            pltpu.SemaphoreType.DMA((3,)),
        ],
        compiler_params=pltpu.CompilerParams(
            vmem_limit_bytes=48 * 1024 * 1024,
            **({"collective_id": 0, "has_side_effects": True} if comm else {}),
        ),
        cost_estimate=pl.CostEstimate(flops=10**10, bytes_accessed=4 * 10**6, transcendentals=10**6),
    )(volume.reshape(shape), taps, offset, upstream.reshape(shape))
    return (
        act.reshape(volume.shape),
        gvol.reshape(volume.shape),
        jnp.transpose(gk.reshape(3, 3, 3, CH, CH), (3, 4, 0, 1, 2)),
        go.reshape(CH),
    )


def solution(mesh):
    cells = mesh.shape["batch"] * mesh.shape["slab"] * PLANES * ROWS * COLS
    split = P("batch", None, "slab", None, None)
    return jax.shard_map(
        functools.partial(layer, True, cells**-0.5),
        mesh=mesh,
        in_specs=(split, P(), P(), split),
        out_specs=(split, split, P(), P()),
        check_vma=False,
    )
```

time: 334 us -> 42.5 us (0.13)
  waiting for transfers between devices: 165 us -> 0 us
  blocking collectives: 81.2 us -> 0 us
  Pallas kernels: 0 us -> 35.1 us
  matrix products: 25.2 us -> 0 us
  local copies, waits for them, and re-layouts: 31 us -> 6.53 us
  between operations: 14.4 us -> 0.65 us
  starting transfers between devices: 11.3 us -> 0 us
  other arithmetic: 5.9 us -> 0 us
    psum x1 -> x0, waiting for transfers between devices: 165 us -> none  [on_device(): lax.psum((local_kernel, local_offset), ('batch', 'slab'))]
    psum x1 -> x0, blocking collectives: 81.2 us -> none  [on_device(): lax.psum((local_kernel, local_offset), ('batch', 'slab'))]
    pallas_call x0 -> x1, Pallas kernels: none -> 35.1 us  [layer(): pl.pallas_call(functools.partial(body, comm, scale), out_shape=(jax.Shape...]
    conv_general_dilated x2 -> x0, matrix products: 16.1 us -> none  [convolve_depth(): lax.conv_general_dilated(field, weights, (1, 1, 1), ((0, 0), (1, 1), (1,...]
    unnamed x31 -> x12, local copies, waits for them, and re-layouts: 18.4 us -> 6.53 us
    ppermute x4 -> x0, starting transfers between devices: 11.2 us -> none  [the longest x2 8.66 us: padded_2(): lax.ppermute(lax.slice_in_dim(block, block.shape[dim] - width, None, axis...]
    dot_general x27 -> x0, matrix products: 9.17 us -> none  [kernel_terms(): jnp.einsum('nodhw,nidhw->oi', grad_pre, window, preferred_element_type=jn...]
  transfers between devices with their start and end apart: 5 -> 0, of which waited for: 2 -> 0; matrix products, arithmetic and copies ran while one was open for 3% -> 0% of each run, Pallas kernels for 0% -> 0%
where the time goes in v1:
time: 42.5 us; the launch traced here: 42.3 us
  Pallas kernels  35.1 us (83%)
  local copies, waits for them, and re-layouts  6.53 us (15%)
  between operations  0.65 us (2%)
    pallas_call x1, Pallas kernels, layer(): pl.pallas_call(functools.partial(body, comm, scale), out_shape=(jax.Shape...  35.1 us
    unnamed x12, local copies, waits for them, and re-layouts  6.53 us

profile of v1, /device:TPU:1, one launch (start us, length us, event | category | flops | bytes accessed | tf_op | source)
XLA Modules:
  0.0 42.3 jit_solution(5735310793310899665)
XLA Ops:
  0.6 0.0 copy-start.3
  0.6 0.6 %copy-done.3 = f32[32]{0:T(128)S(1)} copy-done((f32[32]{0:T(128)S(1)}, f32[32]{0:T(128)}, u32[]{:S(2)}) %copy-start.3) | copy-done | bytes 152
  1.3 0.0 copy-start
  1.3 1.0 %copy-done = bf16[1,32,4,16,128]{4,3,2,1,0:T(8,128)(2,1)S(1)} copy-done((bf16[1,32,4,16,128]{4,3,2,1,0:T(8,128)(2,1)S(1)}, bf16[1,32,4,16,128]{4,3,2,1,0:T(8,128)(2,1)}, u32[]{:S(2)}) %copy-start) | copy-done | bytes 524312
  2.3 0.0 copy-start.1
  2.3 1.0 %copy-done.1 = bf16[1,32,4,16,128]{4,3,2,1,0:T(8,128)(2,1)S(1)} copy-done((bf16[1,32,4,16,128]{4,3,2,1,0:T(8,128)(2,1)S(1)}, bf16[1,32,4,16,128]{4,3,2,1,0:T(8,128)(2,1)}, u32[]{:S(2)}) %copy-start.1) | copy-done | bytes 524312
  3.4 0.0 copy-start.2
  3.4 0.9 %copy-done.2 = bf16[32,32,3,3,3]{1,0,4,3,2:T(8,128)(2,1)S(1)} copy-done((bf16[32,32,3,3,3]{1,0,4,3,2:T(8,128)(2,1)S(1)}, bf16[32,32,3,3,3]{1,0,4,3,2:T(8,128)(2,1)}, u32[]{:S(2)}) %copy-start.2) | copy-done | bytes 55320
  4.3 35.1 %shard_map.75 = (bf16[32,4,16,128]{3,2,1,0:T(8,128)(2,1)S(1)}, bf16[32,4,16,128]{3,2,1,0:T(8,128)(2,1)S(1)}, f32[864,32]{1,0:T(8,128)S(1)}, f32[1,32]{1,0:T(1,128)S(1)}) custom-call(bf16[32,4,16,128]{3,2,1,0:T(8,128)(2,1)S(1)} %bitcast.14, bf16[864,32]{1,0:T(8,128)(2,1)S(1)} %bitcast.16, f32[32]{0:T(128)S(1)} %copy-done.3, bf16[32,4,16,128]{3,2,1,0:T(8,128)(2,1)S(1)} %bitcast.15), custom_call_target="tpu_custom_call" | custom-call | flops 10000000000 | bytes 4000000 | tf_op jit(solution)/shard_map/pallas_call | solution.py:389
  39.4 0.8 %copy.12 = bf16[1,32,4,16,128]{4,3,2,1,0:T(8,128)(2,1)} copy(bf16[1,32,4,16,128]{4,3,2,1,0:T(8,128)(2,1)S(1)} %bitcast.12) | data formatting | bytes 1048576
  40.2 0.8 %copy.13 = bf16[1,32,4,16,128]{4,3,2,1,0:T(8,128)(2,1)} copy(bf16[1,32,4,16,128]{4,3,2,1,0:T(8,128)(2,1)S(1)} %bitcast.11) | data formatting | bytes 1048576
  41.0 0.8 %copy.14 = f32[32,32,3,3,3]{1,0,4,3,2:T(8,128)} copy(f32[32,32,3,3,3]{1,0,4,3,2:T(8,128)S(1)} %bitcast.13) | data formatting | bytes 221184
  41.7 0.5 %copy.15 = f32[32]{0:T(128)} copy(f32[32]{0:T(128)S(1)} %bitcast.17) | data formatting | bytes 256
Async XLA Ops:
  0.6 0.7 %copy-start.3 = (f32[32]{0:T(128)S(1)}, f32[32]{0:T(128)}, u32[]{:S(2)}) copy-start(f32[32]{0:T(128)} %off_ref.1) | copy-start | bytes 388
  1.3 1.0 %copy-start = (bf16[1,32,4,16,128]{4,3,2,1,0:T(8,128)(2,1)S(1)}, bf16[1,32,4,16,128]{4,3,2,1,0:T(8,128)(2,1)}, u32[]{:S(2)}) copy-start(bf16[1,32,4,16,128]{4,3,2,1,0:T(8,128)(2,1)} %param.4) | copy-start | bytes 1572868
  2.3 1.0 %copy-start.1 = (bf16[1,32,4,16,128]{4,3,2,1,0:T(8,128)(2,1)S(1)}, bf16[1,32,4,16,128]{4,3,2,1,0:T(8,128)(2,1)}, u32[]{:S(2)}) copy-start(bf16[1,32,4,16,128]{4,3,2,1,0:T(8,128)(2,1)} %param.7) | copy-start | bytes 1572868
  3.4 0.9 %copy-start.2 = (bf16[32,32,3,3,3]{1,0,4,3,2:T(8,128)(2,1)S(1)}, bf16[32,32,3,3,3]{1,0,4,3,2:T(8,128)(2,1)}, u32[]{:S(2)}) copy-start(bf16[32,32,3,3,3]{1,0,4,3,2:T(8,128)(2,1)} %param.5) | copy-start | bytes 165892

commit v2 on v1

v2 whole, which is shorter than its diff:
```python
import functools

import jax
import jax.numpy as jnp
from jax import lax
from jax.experimental import pallas as pl
from jax.experimental.pallas import tpu as pltpu
from jax.sharding import PartitionSpec as P

MESH = pl.DeviceIdType.MESH
VMEM = 65_500_000
CH = 32
PLANES = 4
ROWS = 16
COLS = 128
BLOCK = 8
WIN = BLOCK + 2
TAPS = 3 * CH
DEEP = WIN * TAPS
GROUPS = 4
RING = 8
MEMBERS = 8 * GROUPS
PACKED = 27 * CH // 4
CHUNKS = PACKED // 8


def banded(pieces, out_ref, plane):
    whole = jnp.concatenate(pieces, axis=1)
    for row in range(BLOCK):
        parts = [whole]
        if row > 0:
            parts.insert(0, jnp.zeros((CH, row * TAPS), jnp.float32))
        if row < BLOCK - 1:
            parts.append(jnp.zeros((CH, (BLOCK - 1 - row) * TAPS), jnp.float32))
        block = jnp.concatenate(parts, axis=1)
        out_ref[plane, row * CH : (row + 1) * CH, :] = block.astype(jnp.bfloat16)


def shifted(values, out_ref, slot, row, flip):
    lane = lax.broadcasted_iota(jnp.int32, (CH, COLS), 1)
    left = jnp.where(lane == 0, 0.0, pltpu.roll(values, 1, 1))
    right = jnp.where(lane == COLS - 1, 0.0, pltpu.roll(values, COLS - 1, 1))
    if flip:
        left, right = right, left
    out_ref[slot, row + 1, 0:CH, :] = left.astype(jnp.bfloat16)
    out_ref[slot, row + 1, CH : 2 * CH, :] = values.astype(jnp.bfloat16)
    out_ref[slot, row + 1, 2 * CH : 3 * CH, :] = right.astype(jnp.bfloat16)


def clear_edges(ref):
    zero = jnp.zeros((TAPS, COLS), jnp.bfloat16)
    for slot in range(PLANES + 2):
        ref[slot, 0] = zero
        ref[slot, ROWS + 1] = zero


def window(ref, slot, half):
    return ref[slot, half * BLOCK : half * BLOCK + WIN].reshape(DEEP, COLS)


def convolve(src_ref, t_ref, terms, sides, out_ref, add):
    for half in range(ROWS // BLOCK):
        acc = None
        for s, slots in terms:
            rhs = jnp.concatenate([window(src_ref, slot, half) for slot in slots], axis=1)
            part = jnp.dot(t_ref[s], rhs, preferred_element_type=jnp.float32)
            acc = part if acc is None else acc + part
        for row in range(BLOCK):
            for place, side in enumerate(sides):
                at = pl.ds(half * BLOCK + row, CH, stride=ROWS)
                value = acc[row * CH : (row + 1) * CH, place * COLS : (place + 1) * COLS]
                if add:
                    value = value + out_ref[side, at, :]
                out_ref[side, at, :] = value


def inner(src_ref, t_ref, out_ref):
    convolve(src_ref, t_ref, [(s, (1 + s, 2 + s)) for s in range(3)], (0, 1), out_ref, False)


def outer_own(src_ref, t_ref, out_ref):
    convolve(src_ref, t_ref, [(1, (1, PLANES))], (0, 1), out_ref, False)
    convolve(src_ref, t_ref, [(2, (2,))], (0,), out_ref, True)
    convolve(src_ref, t_ref, [(0, (PLANES - 1,))], (1,), out_ref, True)


def outer_halo(src_ref, t_ref, out_ref):
    convolve(src_ref, t_ref, [(0, (0,))], (0,), out_ref, True)
    convolve(src_ref, t_ref, [(2, (PLANES + 1,))], (1,), out_ref, True)


def weight_terms(gs_ref, xs_ref, pair, dacc_ref, first):
    lane = lax.broadcasted_iota(jnp.int32, (TAPS, COLS), 1) // CH
    for s in range(3):
        total = [None] * 3
        for half in range(ROWS // BLOCK):
            lhs = jnp.concatenate([window(gs_ref, slot, half) for slot in pair], axis=1)
            rhs = jnp.concatenate(
                [
                    xs_ref[
                        slot + s - 1, 1 + half * BLOCK : 1 + half * BLOCK + BLOCK, CH : 2 * CH, :
                    ].reshape(BLOCK * CH, COLS)
                    for slot in pair
                ],
                axis=1,
            )
            prod = lax.dot_general(
                lhs, rhs, (((1,), (1,)), ((), ())), preferred_element_type=jnp.float32
            )
            for kh in range(3):
                for quad in range(2):
                    picked = None
                    for block in range(4):
                        row = quad * 4 + block + 2 - kh
                        value = prod[row * TAPS : (row + 1) * TAPS, quad * COLS : (quad + 1) * COLS]
                        picked = value if picked is None else jnp.where(lane == block, value, picked)
                    total[kh] = picked if total[kh] is None else total[kh] + picked
        for kh in range(3):
            at = pl.ds((s * 3 + kh) * TAPS, TAPS)
            if first:
                dacc_ref[at, :] = total[kh]
            else:
                dacc_ref[at, :] += total[kh]


class Peers:
    def __init__(self):
        self.batch, self.slab = lax.axis_index("batch"), lax.axis_index("slab")
        self.y, self.z = self.slab // RING, self.slab % RING
        x, core = self.batch // 2, self.batch % 2
        self.mine = self.batch * GROUPS + self.y
        xs = [wrapped(x + d, 4) for d in range(4)]
        cores = [core, 1 - core]
        ys = [wrapped(self.y + d, GROUPS) for d in range(GROUPS)]
        zs = [wrapped(self.z + d, RING) for d in range(RING)]
        group = [(dx, dy, dc) for dx in range(4) for dy in range(GROUPS) for dc in range(2)]
        group = sorted(group[1:], key=lambda t: -(min(t[0], 4 - t[0]) + min(t[1], GROUPS - t[1])))
        self.group = []
        for dx, dy, dc in group:
            batch = xs[dx] * 2 + cores[dc]
            self.group.append((batch * GROUPS + ys[dy], (batch, ys[dy] * RING + self.z)))
        ring = sorted(range(1, RING), key=lambda d: -min(d, RING - d))
        self.ring = [(zs[d], (self.batch, self.y * RING + zs[d])) for d in ring]

        def place(dx=0, dy=0, dz=0, dc=0):
            return (xs[dx] * 2 + cores[dc], ys[dy] * RING + zs[dz])

        self.x_near = [place(dx=1), place(dx=3)]
        self.x_all = [place(dx=1), place(dx=3), place(dx=2)]
        self.y_near = [place(dy=1), place(dy=GROUPS - 1)]
        self.z_near = [place(dz=1), place(dz=RING - 1)]
        self.z_next = [place(dz=2), place(dz=RING - 2)]
        self.twin = place(dc=1)
        self.above = (self.batch, wrapped(self.slab + 1, GROUPS * RING))
        self.below = (self.batch, wrapped(self.slab + GROUPS * RING - 1, GROUPS * RING))


def wrapped(value, count):
    return jnp.where(value >= count, value - count, value)


def remote(src, dst, send, recv, peer):
    return pltpu.make_async_remote_copy(src, dst, send, recv, peer, MESH)


def tell(sem, peers):
    for peer in peers:
        pl.semaphore_signal(sem, 1, device_id=peer, device_id_type=MESH)


def body(
    comm,
    scale,
    vol,
    w_hbm,
    off_hbm,
    up,
    actn,
    gvn,
    res,
    w_ref,
    off_ref,
    vown,
    vhalo,
    upn,
    xf,
    xs,
    gs,
    tf,
    tb,
    pre_in,
    pre_out,
    dacc,
    oacc,
    pay,
    recv1,
    red,
    recv2,
    final,
    local_sem,
    vsend,
    vrecv,
    gsend,
    grecv,
    rsend,
    rrecv,
    known,
):
    if comm:
        peers = Peers()
        group, ring = peers.group, peers.ring
        barrier = pltpu.get_barrier_semaphore()
        near = [peers.above, peers.below] + peers.z_near + peers.y_near + peers.x_near
        near.append(peers.twin)
        tell(barrier, near)

    load_w = pltpu.make_async_copy(w_hbm, w_ref, local_sem.at[4])
    load_w.start()
    load_v = pltpu.make_async_copy(vol, vown, local_sem.at[0])
    load_v.start()
    load_o = pltpu.make_async_copy(off_hbm, off_ref, local_sem.at[5])
    load_o.start()
    load_u = pltpu.make_async_copy(up, upn, local_sem.at[1])
    load_u.start()
    clear_edges(xs)
    clear_edges(gs)

    if comm:
        pl.semaphore_wait(barrier, len(near))
        up_copy = remote(vol.at[:, PLANES - 1], vhalo.at[0], vsend.at[0], vrecv.at[0], peers.above)
        down_copy = remote(vol.at[:, 0], vhalo.at[1], vsend.at[1], vrecv.at[1], peers.below)
        up_copy.start()
        down_copy.start()
        tell(known.at[0], peers.y_near)
        tell(known.at[1], peers.x_near)
        tell(known.at[2], peers.z_near)
        has_below = jnp.where(peers.slab == 0, 0.0, 1.0)
        has_above = jnp.where(peers.slab == GROUPS * RING - 1, 0.0, 1.0)

    load_w.wait()
    taps = w_ref[...].astype(jnp.float32)

    def tap(s, u, k):
        at = ((s * 3 + u) * 3 + k) * CH
        return taps[at : at + CH]

    for s in range(3):
        pieces = [jnp.concatenate([tap(s, u, k) for k in range(3)], axis=1) for u in range(3)]
        banded(pieces, tf, s)

    def spread_volume(slot, values):
        xf[slot] = values.astype(jnp.float32).reshape(CH * ROWS, COLS)
        for row in range(ROWS):
            shifted(xf[slot, pl.ds(row, CH, stride=ROWS), :], xs, slot, row, False)

    if comm:
        for i in range(3):
            pl.semaphore_wait(known.at[i], 2)
        tell(known.at[3], peers.x_all)
        tell(known.at[4], peers.z_next)

    load_v.wait()
    for plane in range(PLANES):
        spread_volume(plane + 1, vown[:, plane])
    load_o.wait()
    load_u.wait()

    def activate(pre, slots, first):
        for side in range(2):
            plane = slots[side] - 1
            for ch in range(CH):
                at = pl.ds(ch * ROWS, ROWS)
                value = pre[side, at, :] + off_ref[ch]
                sig = 0.5 * jnp.tanh(0.5 * value) + 0.5
                actn[ch, plane] = (value * sig).astype(jnp.bfloat16)
                grad = upn[ch, plane].astype(jnp.float32) * sig * (1.0 + value * (1.0 - sig))
                grad = grad.astype(jnp.bfloat16).astype(jnp.float32)
                pre[side, at, :] = grad
                row = jnp.sum(grad, axis=0, keepdims=True)
                if first and side == 0:
                    oacc[ch : ch + 1, :] = row
                else:
                    oacc[ch : ch + 1, :] += row
            for row in range(ROWS):
                shifted(pre[side, pl.ds(row, CH, stride=ROWS), :], gs, plane + 1, row, True)

    inner(xs, tf, pre_in)
    activate(pre_in, (2, 3), True)
    if comm:
        pl.semaphore_wait(known.at[3], 3)
        pl.semaphore_wait(known.at[4], 2)
        tell(known.at[5], [peers.twin])
    weight_terms(gs, xs, (2, 3), dacc, True)
    outer_own(xs, tf, pre_out)

    if comm:
        up_copy.wait_recv()
        down_copy.wait_recv()
        spread_volume(0, vhalo[0].astype(jnp.float32) * has_below)
        spread_volume(PLANES + 1, vhalo[1].astype(jnp.float32) * has_above)
    else:
        for ref in (xs, gs):
            for slot in (0, PLANES + 1):
                ref[slot] = jnp.zeros_like(ref[slot])

    outer_halo(xs, tf, pre_out)
    activate(pre_out, (1, 4), False)
    if comm:

        def edge(slot):
            return gs.at[slot, 1 : ROWS + 1, CH : 2 * CH, :]

        gup = remote(edge(PLANES), edge(0), gsend.at[0], grecv.at[0], peers.above)
        gdown = remote(edge(1), edge(PLANES + 1), gsend.at[1], grecv.at[1], peers.below)
        gup.start()
        gdown.start()
    weight_terms(gs, xs, (1, 4), dacc, False)

    lane = lax.broadcasted_iota(jnp.int32, (PACKED, COLS), 1) // CH
    folded = dacc[...]
    folded = folded + pltpu.roll(folded, 2 * CH, 1)
    folded = folded + pltpu.roll(folded, CH, 1)
    packed = folded[:PACKED]
    for block in range(1, 4):
        packed = jnp.where(lane == block, folded[block * PACKED : (block + 1) * PACKED], packed)
    pay[:CHUNKS] = packed.reshape(CHUNKS, 8, COLS)
    pay[CHUNKS : CHUNKS + 4] = oacc[...].reshape(4, 8, COLS)
    pay[CHUNKS + 4 :] = jnp.zeros((MEMBERS - CHUNKS - 4, 8, COLS), jnp.float32)

    if comm:
        pl.semaphore_wait(known.at[5], 1)
        mine = peers.mine
        for other, peer in group:
            remote(pay.at[other], recv1.at[mine], rsend.at[0], rrecv.at[0], peer).start()
        recv1[mine] = pay[mine]

    turned = taps.T
    for s in range(3):
        pieces = []
        for u in range(3):
            at = ((2 - s) * 3 + 2 - u) * TAPS
            pieces.append(turned[:, at : at + TAPS])
        banded(pieces, tb, s)

    def finish(pre, slots):
        for side in range(2):
            gvn[:, slots[side] - 1] = pre[side].reshape(CH, ROWS, COLS).astype(jnp.bfloat16)

    inner(gs, tb, pre_in)

    if comm:
        some, few = pl.ds(0, MEMBERS - 1), pl.ds(0, RING - 1)
        pltpu.make_async_copy(recv1.at[some], recv1.at[some], rrecv.at[0]).wait()
        red[...] = jnp.sum(recv1[...], axis=0) * scale
        for other, peer in ring:
            remote(red, recv2.at[peers.z], rsend.at[1], rrecv.at[1], peer).start()
        recv2[peers.z] = red[...]

        finish(pre_in, (2, 3))
        outer_own(gs, tb, pre_out)
        gup.wait()
        gdown.wait()
        for slot, keep in ((0, has_below), (PLANES + 1, has_above)):
            for row in range(ROWS):
                value = gs[slot, row + 1, CH : 2 * CH, :].astype(jnp.float32) * keep
                shifted(value, gs, slot, row, True)

        pltpu.make_async_copy(recv2.at[few], recv2.at[few], rrecv.at[1]).wait()
        final[...] = jnp.sum(recv2[...], axis=0)
        for other, peer in group:
            remote(final, res.at[mine], rsend.at[2], rrecv.at[2], peer).start()
        res[mine] = final[...]
    else:
        finish(pre_in, (2, 3))
        outer_own(gs, tb, pre_out)
        res[...] = pay[...] * scale

    outer_halo(gs, tb, pre_out)
    finish(pre_out, (1, 4))
    if comm:
        up_copy.wait_send()
        down_copy.wait_send()
        pltpu.make_async_copy(recv1.at[some], recv1.at[some], rsend.at[0]).wait()
        pltpu.make_async_copy(recv2.at[few], recv2.at[few], rsend.at[1]).wait()
        pltpu.make_async_copy(recv1.at[some], recv1.at[some], rsend.at[2]).wait()
        pltpu.make_async_copy(recv1.at[some], recv1.at[some], rrecv.at[2]).wait()


def write_out(act_in, gvol_in, res, act, gvol, gk, go, gk_ref, go_ref, sem):
    pairs = ((act_in, act), (gvol_in, gvol), (gk_ref, gk), (go_ref, go))
    copies = [pltpu.make_async_copy(src, dst, sem.at[i]) for i, (src, dst) in enumerate(pairs)]
    copies[0].start()
    copies[1].start()
    full = res[:CHUNKS].reshape(PACKED, COLS)
    for block in range(4):
        moved = full if block == 0 else pltpu.roll(full, COLS - block * CH, 1)
        gk_ref[block * PACKED : (block + 1) * PACKED, :] = moved[:, :CH]
    copies[2].start()
    biases = res[CHUNKS : CHUNKS + 4].reshape(CH, COLS)
    go_ref[...] = jnp.sum(biases.T, axis=0, keepdims=True)
    copies[3].start()
    for copy in copies:
        copy.wait()


def layer(comm, scale, volume, kernel, offset, upstream):
    taps = jnp.transpose(kernel, (2, 3, 4, 0, 1)).reshape(27 * CH, CH)
    shape = (CH, PLANES, ROWS, COLS)
    wide = (PLANES + 2, ROWS + 2, TAPS, COLS)
    half, full = jnp.bfloat16, jnp.float32
    hbm = pl.BlockSpec(memory_space=pltpu.HBM)
    vmem = pl.BlockSpec(memory_space=pltpu.VMEM)
    act, gvol, res = pl.pallas_call(
        functools.partial(body, comm, scale),
        out_shape=(
            pltpu.VMEM(shape, half),
            pltpu.VMEM(shape, half),
            pltpu.VMEM((MEMBERS, 8, COLS), full),
        ),
        in_specs=[hbm, hbm, hbm, hbm],
        out_specs=(vmem, vmem, vmem),
        scratch_shapes=[
            pltpu.VMEM((27 * CH, CH), half),
            pltpu.SMEM((CH,), full),
            pltpu.VMEM(shape, half),
            pltpu.VMEM((2, CH, ROWS, COLS), half),
            pltpu.VMEM(shape, half),
            pltpu.VMEM((PLANES + 2, CH * ROWS, COLS), full),
            pltpu.VMEM(wide, half),
            pltpu.VMEM(wide, half),
            pltpu.VMEM((3, BLOCK * CH, DEEP), half),
            pltpu.VMEM((3, BLOCK * CH, DEEP), half),
            pltpu.VMEM((2, CH * ROWS, COLS), full),
            pltpu.VMEM((2, CH * ROWS, COLS), full),
            pltpu.VMEM((27 * CH, COLS), full),
            pltpu.VMEM((CH, COLS), full),
            pltpu.VMEM((MEMBERS, 8, COLS), full),
            pltpu.VMEM((MEMBERS, 8, COLS), full),
            pltpu.VMEM((8, COLS), full),
            pltpu.VMEM((RING, 8, COLS), full),
            pltpu.VMEM((8, COLS), full),
            pltpu.SemaphoreType.DMA((7,)),
            pltpu.SemaphoreType.DMA((2,)),
            pltpu.SemaphoreType.DMA((2,)),
            pltpu.SemaphoreType.DMA((2,)),
            pltpu.SemaphoreType.DMA((2,)),
            pltpu.SemaphoreType.DMA((3,)),
            pltpu.SemaphoreType.DMA((3,)),
            pltpu.SemaphoreType.REGULAR((6,)),
        ],
        compiler_params=pltpu.CompilerParams(
            vmem_limit_bytes=VMEM,
            **({"collective_id": 0, "has_side_effects": True} if comm else {}),
        ),
        cost_estimate=pl.CostEstimate(flops=10**10, bytes_accessed=4 * 10**6, transcendentals=10**6),
    )(volume.reshape(shape), taps, offset, upstream.reshape(shape))
    act, gvol, gk, go = pl.pallas_call(
        write_out,
        out_shape=(
            jax.ShapeDtypeStruct(shape, half),
            jax.ShapeDtypeStruct(shape, half),
            jax.ShapeDtypeStruct((27 * CH, CH), full),
            jax.ShapeDtypeStruct((1, CH), full),
        ),
        in_specs=[vmem, vmem, vmem],
        out_specs=(hbm, hbm, hbm, hbm),
        scratch_shapes=[
            pltpu.VMEM((27 * CH, CH), full),
            pltpu.VMEM((1, CH), full),
            pltpu.SemaphoreType.DMA((4,)),
        ],
        compiler_params=pltpu.CompilerParams(vmem_limit_bytes=8 * 1024 * 1024),
        cost_estimate=pl.CostEstimate(flops=10**5, bytes_accessed=3 * 10**6, transcendentals=0),
    )(act, gvol, res)
    return (
        act.reshape(volume.shape),
        gvol.reshape(volume.shape),
        jnp.transpose(gk.reshape(3, 3, 3, CH, CH), (3, 4, 0, 1, 2)),
        go.reshape(CH),
    )


def solution(mesh):
    cells = mesh.shape["batch"] * mesh.shape["slab"] * PLANES * ROWS * COLS
    split = P("batch", None, "slab", None, None)
    return jax.shard_map(
        functools.partial(layer, True, cells**-0.5),
        mesh=mesh,
        in_specs=(split, P(), P(), split),
        out_specs=(split, split, P(), P()),
        check_vma=False,
    )
```

time: 42.5 us -> 34.9 us (0.82)
  local copies, waits for them, and re-layouts: 6.53 us -> 0 us
  Pallas kernels: 35.1 us -> 34.1 us
    unnamed x12 -> x0, local copies, waits for them, and re-layouts: 6.53 us -> none
    pallas_call x1 -> x2, Pallas kernels: 35.1 us -> 34.1 us  [the longest x1 33 us: layer(): pl.pallas_call(functools.partial(body, comm, scale), out_shape=(pltpu.VME...]
where the time goes in v2:
time: 34.9 us; the launch traced here: 34.8 us
  Pallas kernels  34.1 us (98%)
  between operations  0.64 us (2%)
    pallas_call x1, Pallas kernels, layer(): pl.pallas_call(functools.partial(body, comm, scale), out_shape=(pltpu.VME...  33 us
    pallas_call x1, Pallas kernels, layer(): pl.pallas_call(write_out, out_shape=(jax.ShapeDtypeStruct(shape, half), j...  1.15 us

profile of v2, /device:TPU:1, one launch (start us, length us, event | category | flops | bytes accessed | tf_op | source)
XLA Modules:
  0.0 34.8 jit_solution(18105796973286745701)
XLA Ops:
  0.6 33.0 %shard_map.75 = (bf16[32,4,16,128]{3,2,1,0:T(8,128)(2,1)S(1)}, bf16[32,4,16,128]{3,2,1,0:T(8,128)(2,1)S(1)}, f32[32,8,128]{2,1,0:T(8,128)S(1)}) custom-call(bf16[32,4,16,128]{3,2,1,0:T(8,128)(2,1)} %bitcast.11, bf16[864,32]{1,0:T(8,128)(2,1)} %bitcast.16, f32[32]{0:T(128)} %off_hbm.1, bf16[32,4,16,128]{3,2,1,0:T(8,128)(2,1)} %bitcast.12), custom_call_target="tpu_custom_call" | custom-call | flops 10000000000 | bytes 4000000 | tf_op jit(solution)/shard_map/pallas_call | solution.py:413
  33.6 1.1 %shard_map.76 = (bf16[32,4,16,128]{3,2,1,0:T(8,128)(2,1)}, bf16[32,4,16,128]{3,2,1,0:T(8,128)(2,1)}, f32[864,32]{1,0:T(8,128)}, f32[1,32]{1,0:T(1,128)}) custom-call(bf16[32,4,16,128]{3,2,1,0:T(8,128)(2,1)S(1)} %get-tuple-element.11.act_in, bf16[32,4,16,128]{3,2,1,0:T(8,128)(2,1)S(1)} %get-tuple-element.12.gvol_in, f32[32,8,128]{2,1,0:T(8,128)S(1)} %get-tuple-element.13.res), custom_call_target="tpu_custom_call" | custom-call | flops 100000 | bytes 3000000 | tf_op jit(solution)/shard_map/pallas_call | solution.py:457

commit v3 on v2

--- a/solution.py
+++ b/solution.py
@@ -265,8 +265,8 @@
     load_o.wait()
     load_u.wait()
 
-    def activate(pre, slots, first):
-        for side in range(2):
+    def activate(pre, slots, first, sides=(0, 1)):
+        for side in sides:
             plane = slots[side] - 1
             for ch in range(CH):
                 at = pl.ds(ch * ROWS, ROWS)
@@ -294,26 +294,28 @@
     outer_own(xs, tf, pre_out)
 
     if comm:
+
+        def edge(slot):
+            return gs.at[slot, 1 : ROWS + 1, CH : 2 * CH, :]
+
+        gup = remote(edge(PLANES), edge(0), gsend.at[0], grecv.at[0], peers.above)
+        gdown = remote(edge(1), edge(PLANES + 1), gsend.at[1], grecv.at[1], peers.below)
         up_copy.wait_recv()
-        down_copy.wait_recv()
         spread_volume(0, vhalo[0].astype(jnp.float32) * has_below)
-        spread_volume(PLANES + 1, vhalo[1].astype(jnp.float32) * has_above)
     else:
         for ref in (xs, gs):
             for slot in (0, PLANES + 1):
                 ref[slot] = jnp.zeros_like(ref[slot])
-
-    outer_halo(xs, tf, pre_out)
-    activate(pre_out, (1, 4), False)
-    if comm:
-
-        def edge(slot):
-            return gs.at[slot, 1 : ROWS + 1, CH : 2 * CH, :]
-
-        gup = remote(edge(PLANES), edge(0), gsend.at[0], grecv.at[0], peers.above)
-        gdown = remote(edge(1), edge(PLANES + 1), gsend.at[1], grecv.at[1], peers.below)
+    convolve(xs, tf, [(0, (0,))], (0,), pre_out, True)
+    activate(pre_out, (1, 4), False, (0,))
+    if comm:
+        gdown.start()
+        down_copy.wait_recv()
+        spread_volume(PLANES + 1, vhalo[1].astype(jnp.float32) * has_above)
+    convolve(xs, tf, [(2, (PLANES + 1,))], (1,), pre_out, True)
+    activate(pre_out, (1, 4), False, (1,))
+    if comm:
         gup.start()
-        gdown.start()
     weight_terms(gs, xs, (1, 4), dacc, False)
 
     lane = lax.broadcasted_iota(jnp.int32, (PACKED, COLS), 1) // CH

time: 34.9 us -> 34.5 us (0.989)
    pallas_call x1, Pallas kernels: 33 us -> 32.6 us  [layer(): pl.pallas_call(functools.partial(body, comm, scale), out_shape=(pltpu.VME...]
where the time goes in v3:
time: 34.5 us; the launch traced here: 34.4 us
  Pallas kernels  33.8 us (98%)
  between operations  0.64 us (2%)
    pallas_call x1, Pallas kernels, layer(): pl.pallas_call(functools.partial(body, comm, scale), out_shape=(pltpu.VME...  32.6 us
    pallas_call x1, Pallas kernels, layer(): pl.pallas_call(write_out, out_shape=(jax.ShapeDtypeStruct(shape, half), j...  1.15 us

profile of v3, /device:TPU:1, one launch (start us, length us, event | category | flops | bytes accessed | tf_op | source)
XLA Modules:
  0.0 34.4 jit_solution(12072512664750936893)
XLA Ops:
  0.6 32.6 %shard_map.75 = (bf16[32,4,16,128]{3,2,1,0:T(8,128)(2,1)S(1)}, bf16[32,4,16,128]{3,2,1,0:T(8,128)(2,1)S(1)}, f32[32,8,128]{2,1,0:T(8,128)S(1)}) custom-call(bf16[32,4,16,128]{3,2,1,0:T(8,128)(2,1)} %bitcast.11, bf16[864,32]{1,0:T(8,128)(2,1)} %bitcast.16, f32[32]{0:T(128)} %off_hbm.1, bf16[32,4,16,128]{3,2,1,0:T(8,128)(2,1)} %bitcast.12), custom_call_target="tpu_custom_call" | custom-call | flops 10000000000 | bytes 4000000 | tf_op jit(solution)/shard_map/pallas_call | solution.py:415
  33.3 1.1 %shard_map.76 = (bf16[32,4,16,128]{3,2,1,0:T(8,128)(2,1)}, bf16[32,4,16,128]{3,2,1,0:T(8,128)(2,1)}, f32[864,32]{1,0:T(8,128)}, f32[1,32]{1,0:T(1,128)}) custom-call(bf16[32,4,16,128]{3,2,1,0:T(8,128)(2,1)S(1)} %get-tuple-element.11.act_in, bf16[32,4,16,128]{3,2,1,0:T(8,128)(2,1)S(1)} %get-tuple-element.12.gvol_in, f32[32,8,128]{2,1,0:T(8,128)S(1)} %get-tuple-element.13.res), custom_call_target="tpu_custom_call" | custom-call | flops 100000 | bytes 3000000 | tf_op jit(solution)/shard_map/pallas_call | solution.py:459

commit v4 on v3

--- a/solution.py
+++ b/solution.py
@@ -16,7 +16,7 @@
 BLOCK = 8
 WIN = BLOCK + 2
 TAPS = 3 * CH
-DEEP = WIN * TAPS
+DEEP = 1024
 GROUPS = 4
 RING = 8
 MEMBERS = 8 * GROUPS
@@ -30,10 +30,11 @@
         parts = [whole]
         if row > 0:
             parts.insert(0, jnp.zeros((CH, row * TAPS), jnp.float32))
-        if row < BLOCK - 1:
-            parts.append(jnp.zeros((CH, (BLOCK - 1 - row) * TAPS), jnp.float32))
+        parts.append(jnp.zeros((CH, DEEP - (row + 3) * TAPS), jnp.float32))
         block = jnp.concatenate(parts, axis=1)
-        out_ref[plane, row * CH : (row + 1) * CH, :] = block.astype(jnp.bfloat16)
+        out_ref[row * CH : (row + 1) * CH, plane * DEEP : (plane + 1) * DEEP] = block.astype(
+            jnp.bfloat16
+        )
 
 
 def shifted(values, out_ref, slot, row, flip):
@@ -55,72 +56,95 @@
 
 
 def window(ref, slot, half):
-    return ref[slot, half * BLOCK : half * BLOCK + WIN].reshape(DEEP, COLS)
-
-
-def convolve(src_ref, t_ref, terms, sides, out_ref, add):
+    rows = ref[slot, half * BLOCK : half * BLOCK + WIN].reshape(WIN * TAPS, COLS)
+    return jnp.concatenate([rows, jnp.zeros((DEEP - WIN * TAPS, COLS), jnp.bfloat16)], axis=0)
+
+
+def product(src_ref, t_ref, first, slots, half):
+    sides = [jnp.concatenate([window(src_ref, s, half) for s in group], axis=0) for group in slots]
+    columns = slice(first * DEEP, (first + len(slots[0])) * DEEP)
+    rhs = jnp.concatenate(sides, axis=1)
+    return jnp.dot(t_ref[:, columns], rhs, preferred_element_type=jnp.float32)
+
+
+def put(out_ref, side, half, value, add):
+    for row in range(BLOCK):
+        at = pl.ds(half * BLOCK + row, CH, stride=ROWS)
+        part = value[row * CH : (row + 1) * CH]
+        out_ref[side, at, :] = part + out_ref[side, at, :] if add else part
+
+
+def inner(src_ref, t_ref, out_ref):
     for half in range(ROWS // BLOCK):
-        acc = None
-        for s, slots in terms:
-            rhs = jnp.concatenate([window(src_ref, slot, half) for slot in slots], axis=1)
-            part = jnp.dot(t_ref[s], rhs, preferred_element_type=jnp.float32)
-            acc = part if acc is None else acc + part
-        for row in range(BLOCK):
-            for place, side in enumerate(sides):
-                at = pl.ds(half * BLOCK + row, CH, stride=ROWS)
-                value = acc[row * CH : (row + 1) * CH, place * COLS : (place + 1) * COLS]
-                if add:
-                    value = value + out_ref[side, at, :]
-                out_ref[side, at, :] = value
-
-
-def inner(src_ref, t_ref, out_ref):
-    convolve(src_ref, t_ref, [(s, (1 + s, 2 + s)) for s in range(3)], (0, 1), out_ref, False)
+        acc = product(src_ref, t_ref, 0, [(1, 2, 3), (2, 3, 4)], half)
+        put(out_ref, 0, half, acc[:, :COLS], False)
+        put(out_ref, 1, half, acc[:, COLS:], False)
 
 
 def outer_own(src_ref, t_ref, out_ref):
-    convolve(src_ref, t_ref, [(1, (1, PLANES))], (0, 1), out_ref, False)
-    convolve(src_ref, t_ref, [(2, (2,))], (0,), out_ref, True)
-    convolve(src_ref, t_ref, [(0, (PLANES - 1,))], (1,), out_ref, True)
-
-
-def outer_halo(src_ref, t_ref, out_ref):
-    convolve(src_ref, t_ref, [(0, (0,))], (0,), out_ref, True)
-    convolve(src_ref, t_ref, [(2, (PLANES + 1,))], (1,), out_ref, True)
+    for half in range(ROWS // BLOCK):
+        both = product(src_ref, t_ref, 1, [(1,), (PLANES,)], half)
+        low = both[:, :COLS] + product(src_ref, t_ref, 2, [(2,)], half)
+        high = both[:, COLS:] + product(src_ref, t_ref, 0, [(PLANES - 1,)], half)
+        put(out_ref, 0, half, low, False)
+        put(out_ref, 1, half, high, False)
+
+
+def outer_halo(src_ref, t_ref, out_ref, side):
+    first, slot = (0, 0) if side == 0 else (2, PLANES + 1)
+    for half in range(ROWS // BLOCK):
+        put(out_ref, side, half, product(src_ref, t_ref, first, [(slot,)], half), True)
 
 
 def weight_terms(gs_ref, xs_ref, pair, dacc_ref, first):
-    lane = lax.broadcasted_iota(jnp.int32, (TAPS, COLS), 1) // CH
-    for s in range(3):
-        total = [None] * 3
-        for half in range(ROWS // BLOCK):
-            lhs = jnp.concatenate([window(gs_ref, slot, half) for slot in pair], axis=1)
-            rhs = jnp.concatenate(
-                [
-                    xs_ref[
-                        slot + s - 1, 1 + half * BLOCK : 1 + half * BLOCK + BLOCK, CH : 2 * CH, :
-                    ].reshape(BLOCK * CH, COLS)
-                    for slot in pair
-                ],
-                axis=1,
-            )
-            prod = lax.dot_general(
-                lhs, rhs, (((1,), (1,)), ((), ())), preferred_element_type=jnp.float32
-            )
-            for kh in range(3):
-                for quad in range(2):
-                    picked = None
-                    for block in range(4):
-                        row = quad * 4 + block + 2 - kh
-                        value = prod[row * TAPS : (row + 1) * TAPS, quad * COLS : (quad + 1) * COLS]
-                        picked = value if picked is None else jnp.where(lane == block, value, picked)
-                    total[kh] = picked if total[kh] is None else total[kh] + picked
+    lhs, rhs = [], []
+    pad = jnp.ones((CH * 2, COLS), jnp.bfloat16)
+    for row in range(0, ROWS, 2):
+        for slot in pair:
+            lhs.append(gs_ref[slot, row : row + 4].reshape(4 * TAPS, COLS))
+            sides = [
+                xs_ref[slot + s - 1, row + 1 : row + 3, CH : 2 * CH, :].reshape(2 * CH, COLS)
+                for s in range(3)
+            ]
+            rhs.append(jnp.concatenate(sides + [pad], axis=0))
+    prod = lax.dot_general(
+        jnp.concatenate(lhs, axis=1),
+        jnp.concatenate(rhs, axis=1),
+        (((1,), (1,)), ((), ())),
+        preferred_element_type=jnp.float32,
+    )
+    if first:
+        dacc_ref[...] = prod
+    else:
+        dacc_ref[...] += prod
+
+
+def pack(total):
+    block = lax.broadcasted_iota(jnp.int32, (TAPS, COLS), 1) // CH
+    sides = []
+    for side in range(2):
+        rows = []
         for kh in range(3):
-            at = pl.ds((s * 3 + kh) * TAPS, TAPS)
-            if first:
-                dacc_ref[at, :] = total[kh]
-            else:
-                dacc_ref[at, :] += total[kh]
+            even = total[(2 - kh) * TAPS : (3 - kh) * TAPS, side * COLS : (side + 1) * COLS]
+            odd = total[(3 - kh) * TAPS : (4 - kh) * TAPS, side * COLS : (side + 1) * COLS]
+            rows.append(jnp.where(block % 2 == 0, even, odd))
+        value = jnp.concatenate(rows, axis=0)
+        sides.append(value + pltpu.roll(value, CH, 1))
+    block = lax.broadcasted_iota(jnp.int32, (3 * TAPS, COLS), 1) // CH
+    value = jnp.where(block == 0, pltpu.roll(sides[1], 3 * CH, 1), sides[0])
+    rest = value[PACKED:]
+    moved = [pltpu.roll(rest, shift * CH, 1) for shift in (1, 3, 2)]
+    return jnp.where(block[:PACKED] == 2, jnp.concatenate(moved, axis=0), value[:PACKED])
+
+
+def unpack(full, out_ref):
+    rest = pltpu.roll(full, 2 * CH, 1)[:, :CH]
+    for s, shift in enumerate((3, 1, 0)):
+        at = s * 3 * TAPS
+        value = full if shift == 0 else pltpu.roll(full, shift * CH, 1)
+        out_ref[at : at + PACKED, :] = value[:, :CH]
+        few = 3 * TAPS - PACKED
+        out_ref[at + PACKED : at + 3 * TAPS, :] = rest[s * few : (s + 1) * few]
 
 
 class Peers:
@@ -191,7 +215,6 @@
     pre_in,
     pre_out,
     dacc,
-    oacc,
     pay,
     recv1,
     red,
@@ -265,7 +288,7 @@
     load_o.wait()
     load_u.wait()
 
-    def activate(pre, slots, first, sides=(0, 1)):
+    def activate(pre, slots, sides):
         for side in sides:
             plane = slots[side] - 1
             for ch in range(CH):
@@ -274,18 +297,12 @@
                 sig = 0.5 * jnp.tanh(0.5 * value) + 0.5
                 actn[ch, plane] = (value * sig).astype(jnp.bfloat16)
                 grad = upn[ch, plane].astype(jnp.float32) * sig * (1.0 + value * (1.0 - sig))
-                grad = grad.astype(jnp.bfloat16).astype(jnp.float32)
                 pre[side, at, :] = grad
-                row = jnp.sum(grad, axis=0, keepdims=True)
-                if first and side == 0:
-                    oacc[ch : ch + 1, :] = row
-                else:
-                    oacc[ch : ch + 1, :] += row
             for row in range(ROWS):
                 shifted(pre[side, pl.ds(row, CH, stride=ROWS), :], gs, plane + 1, row, True)
 
     inner(xs, tf, pre_in)
-    activate(pre_in, (2, 3), True)
+    activate(pre_in, (2, 3), (0, 1))
     if comm:
         pl.semaphore_wait(known.at[3], 3)
         pl.semaphore_wait(known.at[4], 2)
@@ -306,27 +323,22 @@
         for ref in (xs, gs):
             for slot in (0, PLANES + 1):
                 ref[slot] = jnp.zeros_like(ref[slot])
-    convolve(xs, tf, [(0, (0,))], (0,), pre_out, True)
-    activate(pre_out, (1, 4), False, (0,))
+    outer_halo(xs, tf, pre_out, 0)
+    activate(pre_out, (1, 4), (0,))
     if comm:
         gdown.start()
         down_copy.wait_recv()
         spread_volume(PLANES + 1, vhalo[1].astype(jnp.float32) * has_above)
-    convolve(xs, tf, [(2, (PLANES + 1,))], (1,), pre_out, True)
-    activate(pre_out, (1, 4), False, (1,))
+    outer_halo(xs, tf, pre_out, 1)
+    activate(pre_out, (1, 4), (1,))
     if comm:
         gup.start()
     weight_terms(gs, xs, (1, 4), dacc, False)
 
-    lane = lax.broadcasted_iota(jnp.int32, (PACKED, COLS), 1) // CH
-    folded = dacc[...]
-    folded = folded + pltpu.roll(folded, 2 * CH, 1)
-    folded = folded + pltpu.roll(folded, CH, 1)
-    packed = folded[:PACKED]
-    for block in range(1, 4):
-        packed = jnp.where(lane == block, folded[block * PACKED : (block + 1) * PACKED], packed)
+    packed = pack(dacc[...])
     pay[:CHUNKS] = packed.reshape(CHUNKS, 8, COLS)
-    pay[CHUNKS : CHUNKS + 4] = oacc[...].reshape(4, 8, COLS)
+    sums = [dacc[row * TAPS + CH : row * TAPS + 2 * CH, COLS:] for row in (1, 2)]
+    pay[CHUNKS : CHUNKS + 4] = (sums[0] + sums[1]).reshape(4, 8, COLS)
     pay[CHUNKS + 4 :] = jnp.zeros((MEMBERS - CHUNKS - 4, 8, COLS), jnp.float32)
 
     if comm:
@@ -377,7 +389,8 @@
         outer_own(gs, tb, pre_out)
         res[...] = pay[...] * scale
 
-    outer_halo(gs, tb, pre_out)
+    outer_halo(gs, tb, pre_out, 0)
+    outer_halo(gs, tb, pre_out, 1)
     finish(pre_out, (1, 4))
     if comm:
         up_copy.wait_send()
@@ -393,13 +406,10 @@
     copies = [pltpu.make_async_copy(src, dst, sem.at[i]) for i, (src, dst) in enumerate(pairs)]
     copies[0].start()
     copies[1].start()
-    full = res[:CHUNKS].reshape(PACKED, COLS)
-    for block in range(4):
-        moved = full if block == 0 else pltpu.roll(full, COLS - block * CH, 1)
-        gk_ref[block * PACKED : (block + 1) * PACKED, :] = moved[:, :CH]
+    unpack(res[:CHUNKS].reshape(PACKED, COLS), gk_ref)
     copies[2].start()
     biases = res[CHUNKS : CHUNKS + 4].reshape(CH, COLS)
-    go_ref[...] = jnp.sum(biases.T, axis=0, keepdims=True)
+    go_ref[...] = biases.T[2 * CH : 2 * CH + 1, :]
     copies[3].start()
     for copy in copies:
         copy.wait()
@@ -430,12 +440,11 @@
             pltpu.VMEM((PLANES + 2, CH * ROWS, COLS), full),
             pltpu.VMEM(wide, half),
             pltpu.VMEM(wide, half),
-            pltpu.VMEM((3, BLOCK * CH, DEEP), half),
-            pltpu.VMEM((3, BLOCK * CH, DEEP), half),
+            pltpu.VMEM((BLOCK * CH, 3 * DEEP), half),
+            pltpu.VMEM((BLOCK * CH, 3 * DEEP), half),
             pltpu.VMEM((2, CH * ROWS, COLS), full),
             pltpu.VMEM((2, CH * ROWS, COLS), full),
-            pltpu.VMEM((27 * CH, COLS), full),
-            pltpu.VMEM((CH, COLS), full),
+            pltpu.VMEM((4 * TAPS, 2 * COLS), full),
             pltpu.VMEM((MEMBERS, 8, COLS), full),
             pltpu.VMEM((MEMBERS, 8, COLS), full),
             pltpu.VMEM((8, COLS), full),

time: 34.5 us -> 33.9 us (0.983)
  Pallas kernels: 33.8 us -> 33.2 us
    pallas_call x1, Pallas kernels: 32.6 us -> 32 us  [layer(): pl.pallas_call(functools.partial(body, comm, scale), out_shape=(pltpu.VME...]
where the time goes in v4:
time: 33.9 us; the launch traced here: 33.8 us
  Pallas kernels  33.2 us (98%)
  between operations  0.64 us (2%)
    pallas_call x1, Pallas kernels, layer(): pl.pallas_call(functools.partial(body, comm, scale), out_shape=(pltpu.VME...  32 us
    pallas_call x1, Pallas kernels, layer(): pl.pallas_call(write_out, out_shape=(jax.ShapeDtypeStruct(shape, half), j...  1.15 us

profile of v4, /device:TPU:1, one launch (start us, length us, event | category | flops | bytes accessed | tf_op | source)
XLA Modules:
  0.0 33.8 jit_solution(7027053439086275550)
XLA Ops:
  0.6 32.0 %shard_map.75 = (bf16[32,4,16,128]{3,2,1,0:T(8,128)(2,1)S(1)}, bf16[32,4,16,128]{3,2,1,0:T(8,128)(2,1)S(1)}, f32[32,8,128]{2,1,0:T(8,128)S(1)}) custom-call(bf16[32,4,16,128]{3,2,1,0:T(8,128)(2,1)} %bitcast.11, bf16[864,32]{1,0:T(8,128)(2,1)} %bitcast.16, f32[32]{0:T(128)} %off_hbm.1, bf16[32,4,16,128]{3,2,1,0:T(8,128)(2,1)} %bitcast.12), custom_call_target="tpu_custom_call" | custom-call | flops 10000000000 | bytes 4000000 | tf_op jit(solution)/shard_map/pallas_call | solution.py:425
  32.6 1.1 %shard_map.76 = (bf16[32,4,16,128]{3,2,1,0:T(8,128)(2,1)}, bf16[32,4,16,128]{3,2,1,0:T(8,128)(2,1)}, f32[864,32]{1,0:T(8,128)}, f32[1,32]{1,0:T(1,128)}) custom-call(bf16[32,4,16,128]{3,2,1,0:T(8,128)(2,1)S(1)} %get-tuple-element.11.act_in, bf16[32,4,16,128]{3,2,1,0:T(8,128)(2,1)S(1)} %get-tuple-element.12.gvol_in, f32[32,8,128]{2,1,0:T(8,128)S(1)} %get-tuple-element.13.res), custom_call_target="tpu_custom_call" | custom-call | flops 100000 | bytes 3000000 | tf_op jit(solution)/shard_map/pallas_call | solution.py:468

commit v5 on v4

--- a/solution.py
+++ b/solution.py
@@ -276,12 +276,6 @@
         for row in range(ROWS):
             shifted(xf[slot, pl.ds(row, CH, stride=ROWS), :], xs, slot, row, False)
 
-    if comm:
-        for i in range(3):
-            pl.semaphore_wait(known.at[i], 2)
-        tell(known.at[3], peers.x_all)
-        tell(known.at[4], peers.z_next)
-
     load_v.wait()
     for plane in range(PLANES):
         spread_volume(plane + 1, vown[:, plane])
@@ -302,13 +296,18 @@
                 shifted(pre[side, pl.ds(row, CH, stride=ROWS), :], gs, plane + 1, row, True)
 
     inner(xs, tf, pre_in)
+    if comm:
+        for i in range(3):
+            pl.semaphore_wait(known.at[i], 2)
+        tell(known.at[3], peers.x_all)
+        tell(known.at[4], peers.z_next)
     activate(pre_in, (2, 3), (0, 1))
+    weight_terms(gs, xs, (2, 3), dacc, True)
+    outer_own(xs, tf, pre_out)
     if comm:
         pl.semaphore_wait(known.at[3], 3)
         pl.semaphore_wait(known.at[4], 2)
         tell(known.at[5], [peers.twin])
-    weight_terms(gs, xs, (2, 3), dacc, True)
-    outer_own(xs, tf, pre_out)
 
     if comm:
 

time: 33.9 us -> 33.1 us (0.976)
  Pallas kernels: 33.2 us -> 32.3 us
    pallas_call x1, Pallas kernels: 32 us -> 31.2 us  [layer(): pl.pallas_call(functools.partial(body, comm, scale), out_shape=(pltpu.VME...]
where the time goes in v5:
time: 33.1 us; the launch traced here: 33 us
  Pallas kernels  32.3 us (98%)
  between operations  0.64 us (2%)
    pallas_call x1, Pallas kernels, layer(): pl.pallas_call(functools.partial(body, comm, scale), out_shape=(pltpu.VME...  31.2 us
    pallas_call x1, Pallas kernels, layer(): pl.pallas_call(write_out, out_shape=(jax.ShapeDtypeStruct(shape, half), j...  1.15 us

profile of v5, /device:TPU:1, one launch (start us, length us, event | category | flops | bytes accessed | tf_op | source)
XLA Modules:
  0.0 33.0 jit_solution(15720646523692560101)
XLA Ops:
  0.6 31.2 %shard_map.75 = (bf16[32,4,16,128]{3,2,1,0:T(8,128)(2,1)S(1)}, bf16[32,4,16,128]{3,2,1,0:T(8,128)(2,1)S(1)}, f32[32,8,128]{2,1,0:T(8,128)S(1)}) custom-call(bf16[32,4,16,128]{3,2,1,0:T(8,128)(2,1)} %bitcast.11, bf16[864,32]{1,0:T(8,128)(2,1)} %bitcast.16, f32[32]{0:T(128)} %off_hbm.1, bf16[32,4,16,128]{3,2,1,0:T(8,128)(2,1)} %bitcast.12), custom_call_target="tpu_custom_call" | custom-call | flops 10000000000 | bytes 4000000 | tf_op jit(solution)/shard_map/pallas_call | solution.py:424
  31.8 1.1 %shard_map.76 = (bf16[32,4,16,128]{3,2,1,0:T(8,128)(2,1)}, bf16[32,4,16,128]{3,2,1,0:T(8,128)(2,1)}, f32[864,32]{1,0:T(8,128)}, f32[1,32]{1,0:T(1,128)}) custom-call(bf16[32,4,16,128]{3,2,1,0:T(8,128)(2,1)S(1)} %get-tuple-element.11.act_in, bf16[32,4,16,128]{3,2,1,0:T(8,128)(2,1)S(1)} %get-tuple-element.12.gvol_in, f32[32,8,128]{2,1,0:T(8,128)S(1)} %get-tuple-element.13.res), custom_call_target="tpu_custom_call" | custom-call | flops 100000 | bytes 3000000 | tf_op jit(solution)/shard_map/pallas_call | solution.py:467

commit v6 on v5

--- a/solution.py
+++ b/solution.py
@@ -237,9 +237,14 @@
         near.append(peers.twin)
         tell(barrier, near)
 
+    inside = pl.ds(1, PLANES - 2)
+    load_top = pltpu.make_async_copy(vol.at[:, PLANES - 1], vown.at[:, PLANES - 1], local_sem.at[2])
+    load_top.start()
+    load_low = pltpu.make_async_copy(vol.at[:, 0], vown.at[:, 0], local_sem.at[3])
+    load_low.start()
     load_w = pltpu.make_async_copy(w_hbm, w_ref, local_sem.at[4])
     load_w.start()
-    load_v = pltpu.make_async_copy(vol, vown, local_sem.at[0])
+    load_v = pltpu.make_async_copy(vol.at[:, inside], vown.at[:, inside], local_sem.at[0])
     load_v.start()
     load_o = pltpu.make_async_copy(off_hbm, off_ref, local_sem.at[5])
     load_o.start()
@@ -250,8 +255,10 @@
 
     if comm:
         pl.semaphore_wait(barrier, len(near))
-        up_copy = remote(vol.at[:, PLANES - 1], vhalo.at[0], vsend.at[0], vrecv.at[0], peers.above)
-        down_copy = remote(vol.at[:, 0], vhalo.at[1], vsend.at[1], vrecv.at[1], peers.below)
+        load_top.wait()
+        load_low.wait()
+        up_copy = remote(vown.at[:, PLANES - 1], vhalo.at[0], vsend.at[0], vrecv.at[0], peers.above)
+        down_copy = remote(vown.at[:, 0], vhalo.at[1], vsend.at[1], vrecv.at[1], peers.below)
         up_copy.start()
         down_copy.start()
         tell(known.at[0], peers.y_near)
@@ -259,6 +266,9 @@
         tell(known.at[2], peers.z_near)
         has_below = jnp.where(peers.slab == 0, 0.0, 1.0)
         has_above = jnp.where(peers.slab == GROUPS * RING - 1, 0.0, 1.0)
+    else:
+        load_top.wait()
+        load_low.wait()
 
     load_w.wait()
     taps = w_ref[...].astype(jnp.float32)

time: 33.1 us -> 32.9 us (level)
  no operation moved by 1% of the time
where the time goes in v6:
time: 32.9 us; the launch traced here: 32.8 us
  Pallas kernels  32.2 us (98%)
  between operations  0.64 us (2%)
    pallas_call x1, Pallas kernels, layer(): pl.pallas_call(functools.partial(body, comm, scale), out_shape=(pltpu.VME...  31 us
    pallas_call x1, Pallas kernels, layer(): pl.pallas_call(write_out, out_shape=(jax.ShapeDtypeStruct(shape, half), j...  1.15 us

profile of v6, /device:TPU:1, one launch (start us, length us, event | category | flops | bytes accessed | tf_op | source)
XLA Modules:
  0.0 32.8 jit_solution(1640735538238706362)
XLA Ops:
  0.6 31.0 %shard_map.75 = (bf16[32,4,16,128]{3,2,1,0:T(8,128)(2,1)S(1)}, bf16[32,4,16,128]{3,2,1,0:T(8,128)(2,1)S(1)}, f32[32,8,128]{2,1,0:T(8,128)S(1)}) custom-call(bf16[32,4,16,128]{3,2,1,0:T(8,128)(2,1)} %bitcast.11, bf16[864,32]{1,0:T(8,128)(2,1)} %bitcast.16, f32[32]{0:T(128)} %off_hbm.1, bf16[32,4,16,128]{3,2,1,0:T(8,128)(2,1)} %bitcast.12), custom_call_target="tpu_custom_call" | custom-call | flops 10000000000 | bytes 4000000 | tf_op jit(solution)/shard_map/pallas_call | solution.py:434
  31.7 1.1 %shard_map.76 = (bf16[32,4,16,128]{3,2,1,0:T(8,128)(2,1)}, bf16[32,4,16,128]{3,2,1,0:T(8,128)(2,1)}, f32[864,32]{1,0:T(8,128)}, f32[1,32]{1,0:T(1,128)}) custom-call(bf16[32,4,16,128]{3,2,1,0:T(8,128)(2,1)S(1)} %get-tuple-element.11.act_in, bf16[32,4,16,128]{3,2,1,0:T(8,128)(2,1)S(1)} %get-tuple-element.12.gvol_in, f32[32,8,128]{2,1,0:T(8,128)S(1)} %get-tuple-element.13.res), custom_call_target="tpu_custom_call" | custom-call | flops 100000 | bytes 3000000 | tf_op jit(solution)/shard_map/pallas_call | solution.py:477

commit v7 on v6

--- a/solution.py
+++ b/solution.py
@@ -229,6 +229,11 @@
     rrecv,
     known,
 ):
+    load_top = pltpu.make_async_copy(vol.at[:, PLANES - 1], vown.at[:, PLANES - 1], local_sem.at[2])
+    load_top.start()
+    load_low = pltpu.make_async_copy(vol.at[:, 0], vown.at[:, 0], local_sem.at[3])
+    load_low.start()
+
     if comm:
         peers = Peers()
         group, ring = peers.group, peers.ring
@@ -238,10 +243,6 @@
         tell(barrier, near)
 
     inside = pl.ds(1, PLANES - 2)
-    load_top = pltpu.make_async_copy(vol.at[:, PLANES - 1], vown.at[:, PLANES - 1], local_sem.at[2])
-    load_top.start()
-    load_low = pltpu.make_async_copy(vol.at[:, 0], vown.at[:, 0], local_sem.at[3])
-    load_low.start()
     load_w = pltpu.make_async_copy(w_hbm, w_ref, local_sem.at[4])
     load_w.start()
     load_v = pltpu.make_async_copy(vol.at[:, inside], vown.at[:, inside], local_sem.at[0])
@@ -250,8 +251,6 @@
     load_o.start()
     load_u = pltpu.make_async_copy(up, upn, local_sem.at[1])
     load_u.start()
-    clear_edges(xs)
-    clear_edges(gs)
 
     if comm:
         pl.semaphore_wait(barrier, len(near))
@@ -270,6 +269,8 @@
         load_top.wait()
         load_low.wait()
 
+    clear_edges(xs)
+    clear_edges(gs)
     load_w.wait()
     taps = w_ref[...].astype(jnp.float32)
 

time: 32.9 us -> 32.9 us (level)
  no operation moved by 1% of the time
where the time goes in v7:
time: 32.9 us; the launch traced here: 32.8 us
  Pallas kernels  32.1 us (98%)
  between operations  0.64 us (2%)
    pallas_call x1, Pallas kernels, layer(): pl.pallas_call(functools.partial(body, comm, scale), out_shape=(pltpu.VME...  31 us
    pallas_call x1, Pallas kernels, layer(): pl.pallas_call(write_out, out_shape=(jax.ShapeDtypeStruct(shape, half), j...  1.15 us

profile of v7, /device:TPU:1, one launch (start us, length us, event | category | flops | bytes accessed | tf_op | source)
XLA Modules:
  0.0 32.8 jit_solution(9642924474346968749)
XLA Ops:
  0.6 31.0 %shard_map.75 = (bf16[32,4,16,128]{3,2,1,0:T(8,128)(2,1)S(1)}, bf16[32,4,16,128]{3,2,1,0:T(8,128)(2,1)S(1)}, f32[32,8,128]{2,1,0:T(8,128)S(1)}) custom-call(bf16[32,4,16,128]{3,2,1,0:T(8,128)(2,1)} %bitcast.11, bf16[864,32]{1,0:T(8,128)(2,1)} %bitcast.16, f32[32]{0:T(128)} %off_hbm.1, bf16[32,4,16,128]{3,2,1,0:T(8,128)(2,1)} %bitcast.12), custom_call_target="tpu_custom_call" | custom-call | flops 10000000000 | bytes 4000000 | tf_op jit(solution)/shard_map/pallas_call | solution.py:435
  31.6 1.1 %shard_map.76 = (bf16[32,4,16,128]{3,2,1,0:T(8,128)(2,1)}, bf16[32,4,16,128]{3,2,1,0:T(8,128)(2,1)}, f32[864,32]{1,0:T(8,128)}, f32[1,32]{1,0:T(1,128)}) custom-call(bf16[32,4,16,128]{3,2,1,0:T(8,128)(2,1)S(1)} %get-tuple-element.11.act_in, bf16[32,4,16,128]{3,2,1,0:T(8,128)(2,1)S(1)} %get-tuple-element.12.gvol_in, f32[32,8,128]{2,1,0:T(8,128)S(1)} %get-tuple-element.13.res), custom_call_target="tpu_custom_call" | custom-call | flops 100000 | bytes 3000000 | tf_op jit(solution)/shard_map/pallas_call | solution.py:478
